TPU v7x, 32 devices: a whole 2x2x4 slice. The times are simulated.
32 devices in a mesh: dp: 4 (over z), tensor: 4 (over y, x), section: 2 (over core).
Axes of the slice: x: 2, y: 2, z: 4, core: 2. Of those that a mesh axis runs over, the one named last changes fastest.
Arguments:
- grad_mat: bfloat16 [4, 4, 1600, 4800], P('dp', 'tensor', 'section'), may hold values from -6 to 6
- grad_vec: bfloat16 [4, 20800], P('dp'), may hold values from -6 to 6
- master_mat: float32 [4, 2, 4, 200, 4800], P('tensor', 'section', 'dp'), may hold values from -9 to 9
- first_mat: float32 [4, 2, 4, 200, 4800], P('tensor', 'section', 'dp'), may hold values from -4 to 4
- second_mat: float32 [4, 2, 4, 200, 4800], P('tensor', 'section', 'dp'), may hold values from 0.001 to 0.1
- master_vec: float32 [4, 5200], P('dp'), may hold values from -6 to 6
- first_vec: float32 [4, 5200], P('dp'), may hold values from -4 to 4
- second_vec: float32 [4, 5200], P('dp'), may hold values from 0.001 to 0.1
Outputs:
- weights_mat: bfloat16 [4, 1600, 4800], P('tensor', 'section')
- weights_vec: bfloat16 [20800], replicated
- new_master_mat: float32 [4, 2, 4, 200, 4800], P('tensor', 'section', 'dp')
- new_first_mat: float32 [4, 2, 4, 200, 4800], P('tensor', 'section', 'dp')
- new_second_mat: float32 [4, 2, 4, 200, 4800], P('tensor', 'section', 'dp')
- new_master_vec: float32 [4, 5200], P('dp')
- new_first_vec: float32 [4, 5200], P('dp')
- new_second_vec: float32 [4, 5200], P('dp')
All inputs are finite; a program needn't handle non-finite values.
Results may differ from a plain program's by a relative error of at most 0.0004.
Values may be sent and summed in bfloat16 or wider, within the bound.
A program may use at most 128 MiB of HBM per device.

v0:
```python
import jax
import jax.numpy as jnp
from jax import lax
from jax.sharding import PartitionSpec as P

D = 1600
FF = 6400
STEP = 10


BETA_ONE = 0.9
BETA_TWO = 0.999
EPSILON = 1e-06
LEARN_RATE = 0.25
DECAY_MAT = 0.01


def adam_direction(gradient, master, first, second, decay):
    first_new = BETA_ONE * first + (1.0 - BETA_ONE) * gradient
    second_new = BETA_TWO * second + (1.0 - BETA_TWO) * gradient * gradient
    corr_one = 1.0 - BETA_ONE**STEP
    corr_two = 1.0 - BETA_TWO**STEP
    direction = first_new / corr_one / (jnp.sqrt(second_new / corr_two) + EPSILON) + decay * master
    return (first_new, second_new, direction)


def segment_masks(position, bounds):
    lower = jnp.array(bounds[:-1], dtype=jnp.int32)[:, None]
    upper = jnp.array(bounds[1:], dtype=jnp.int32)[:, None]
    return ((position[None, :] >= lower) & (position[None, :] < upper)).astype(jnp.float32)


def local(grad_mat, grad_vec, master_mat, first_mat, second_mat, master_vec, first_vec, second_vec):
    tensor_count = lax.axis_size("tensor")
    section_rows = grad_mat.shape[2]
    columns = grad_mat.shape[3]
    vec_length = grad_vec.shape[1]
    state_shape = master_mat.shape
    vec_shape = master_vec.shape
    owned_vec = vec_shape[1]
    master = master_mat.reshape(-1, columns)
    master_v = master_vec.reshape(owned_vec)
    bounds_mat = [
        0,
        3 * D // tensor_count,
        4 * D // tensor_count,
        (4 * D + FF) // tensor_count,
        columns,
    ]
    masks_mat = segment_masks(lax.iota(jnp.int32, columns), bounds_mat)
    bounds_vec = [0, D, 2 * D, 5 * D, 6 * D, 7 * D, 8 * D, 8 * D + FF, 9 * D + FF]
    vec_index = lax.axis_index("dp") * owned_vec + lax.iota(jnp.int32, owned_vec)
    masks_vec = segment_masks(vec_index, bounds_vec)
    weight_mat_sq = jnp.sum(masks_mat * jnp.sum(master * master, axis=0)[None, :], axis=1)
    weight_vec_sq = jnp.sum(masks_vec * (master_v * master_v)[None, :], axis=1)
    local_grad = grad_mat.reshape(section_rows, columns).astype(jnp.float32)
    local_vec = grad_vec.reshape(vec_length).astype(jnp.float32)
    gradient, gradient_v = (
        lax.psum_scatter(local_grad, "dp", scatter_dimension=0, tiled=True),
        lax.psum_scatter(local_vec, "dp", scatter_dimension=0, tiled=True),
    )
    first_new, second_new, direction = adam_direction(
        gradient, master, first_mat.reshape(-1, columns), second_mat.reshape(-1, columns), DECAY_MAT
    )
    first_v, second_v, direction_v = adam_direction(
        gradient_v, master_v, first_vec.reshape(owned_vec), second_vec.reshape(owned_vec), 0.0
    )
    update_mat_sq = jnp.sum(masks_mat * jnp.sum(direction * direction, axis=0)[None, :], axis=1)
    update_vec_sq = jnp.sum(masks_vec * (direction_v * direction_v)[None, :], axis=1)
    wsum_mat, usum_mat = lax.psum((weight_mat_sq, update_mat_sq), ("dp", "tensor", "section"))
    wsum_vec, usum_vec = lax.psum((weight_vec_sq, update_vec_sq), "dp")
    ratio_mat = jnp.sqrt(wsum_mat) / jnp.sqrt(usum_mat)
    ratio_vec = jnp.sqrt(wsum_vec) / jnp.sqrt(usum_vec)
    ratio_cols = jnp.sum(masks_mat * ratio_mat[:, None], axis=0)
    ratio_entries = jnp.sum(masks_vec * ratio_vec[:, None], axis=0)
    master_new = master - LEARN_RATE * ratio_cols[None, :] * direction
    master_v_new = master_v - LEARN_RATE * ratio_entries * direction_v
    weights_mat, weights_vec = (
        lax.all_gather(master_new.astype(jnp.bfloat16), "dp", axis=0, tiled=True),
        lax.all_gather(master_v_new.astype(jnp.bfloat16), "dp", axis=0, tiled=True),
    )
    return (
        weights_mat.reshape(1, section_rows, columns),
        weights_vec,
        master_new.reshape(state_shape),
        first_new.reshape(state_shape),
        second_new.reshape(state_shape),
        master_v_new.reshape(vec_shape),
        first_v.reshape(vec_shape),
        second_v.reshape(vec_shape),
    )


def solution(mesh):
    in_specs = (
        P("dp", "tensor", "section", None),
        P("dp", None),
        P("tensor", "section", "dp", None, None),
        P("tensor", "section", "dp", None, None),
        P("tensor", "section", "dp", None, None),
        P("dp", None),
        P("dp", None),
        P("dp", None),
    )
    out_specs = (
        P("tensor", "section", None),
        P(),
        P("tensor", "section", "dp", None, None),
        P("tensor", "section", "dp", None, None),
        P("tensor", "section", "dp", None, None),
        P("dp", None),
        P("dp", None),
        P("dp", None),
    )
    return jax.shard_map(local, mesh=mesh, in_specs=in_specs, out_specs=out_specs, check_vma=False)
```

profile of v0, /device:TPU:0, one launch (start us, length us, event | category | flops | bytes accessed | tf_op | source)
XLA Modules:
  0.0 493.4 jit_solution(16225951103398537851)
XLA Ops:
  7.2 9.8 %bitcast_convert_fusion = f32[800,4800]{1,0:T(8,128)} fusion(bf16[1,1,800,4800]{3,2,1,0:T(8,128)(2,1)} %param.12), kind=kLoop, calls=%fused_computation | loop fusion | flops 3840000 | bytes 23040000 | tf_op jit(solution)/shard_map/convert_element_type | solution.py:56
  17.1 0.8 copy-done
  17.9 0.9 convert_reduce_fusion
  18.8 0.0 all-gather.2.cloned.1.call-start
  18.9 261.4 %reduce-scatter.2.cloned.1.call-done = f32[200,4800]{1,0:T(8,128)} async-done(((f32[800,4800]{1,0:T(8,128)}), f32[200,4800]{1,0:T(8,128)}) %reduce-scatter.2.cloned.1.call-update) | async-done | bytes 3840016 | tf_op jit(solution)/shard_map/reduce_scatter | solution.py:59
  280.2 10.3 %multiply_reduce_fusion = (f32[4800]{0:T(1024)S(1)}, f32[200,4800]{1,0:T(8,128)}, f32[1,1,1,200,4800]{4,3,2,1,0:T(8,128)}, f32[1,1,1,200,4800]{4,3,2,1,0:T(8,128)}, f32[4800]{0:T(1024)S(1)}) fusion(f32[1,1,1,200,4800]{4,3,2,1,0:T(8,128)} %param.14, f32[200,4800]{1,0:T(8,128)} %reduce-scatter.2.cloned.1.call-done, f32[1,1,1,200,4800]{4,3,2,1,0:T(8,128)} %param.16, ...), kind=kLoop, calls=%fused_computation.9 | loop fusion | flops 16310400 | bytes 26918400 | tf_op jit(solution)/shard_map/reduce_sum | solution.py:68
  290.6 0.3 select_reduce_fusion.5
  290.9 41.4 %all-reduce.2 = (f32[4]{0:T(128)S(1)}, f32[4]{0:T(128)S(1)}) all-reduce(f32[4]{0:T(128)S(1)} %get-tuple-element.13, f32[4]{0:T(128)S(1)} %get-tuple-element.12), channel_id=1, replica_groups=mesh['dp'=4,'tensor'=4,'section'=2] {'dp','tensor','section'}, use_global_device_ids=true, to_apply=%region_6.0 | all-reduce | flops 8 | bytes 64 | tf_op jit(solution)/shard_map/psum | solution.py:70
  332.2 0.1 select_reduce_fusion.3
  332.5 6.3 %fusion.3 = (f32[1,1,1,200,4800]{4,3,2,1,0:T(8,128)}, bf16[200,4800]{1,0:T(8,128)(2,1)}) fusion(f32[200,4800]{1,0:T(8,128)} %get-tuple-element.24, f32[4800]{0:T(1024)S(1)} %broadcast_multiply_fusion, f32[1,1,1,200,4800]{4,3,2,1,0:T(8,128)} %param.14), kind=kLoop, calls=%fused_computation.10 | loop fusion | flops 2880000 | bytes 13459200 | tf_op jit(solution)/shard_map/reshape | solution.py:85
  338.8 0.6 fusion.13
  340.8 0.1 multiply_reduce_fusion.3
  340.9 0.1 multiply_reduce_fusion.1
  341.0 0.9 fusion.9
  341.9 0.3 select_reduce_fusion.2
  342.2 10.7 %all-reduce.3 = (f32[8]{0:T(128)S(1)}, f32[8]{0:T(128)S(1)}) all-reduce(f32[8]{0:T(128)S(1)} %get-tuple-element.9, f32[8]{0:T(128)S(1)} %get-tuple-element.8), channel_id=1, replica_groups=mesh['dp'=4,'tensor'=4,'section'=2] {'dp'}, use_global_device_ids=true, to_apply=%region_12.0 | all-reduce | flops 16 | bytes 128 | tf_op jit(solution)/shard_map/psum | solution.py:71
  352.9 0.6 reshape.85
  353.5 0.6 reshape.86
  354.2 0.1 select_reduce_fusion
  354.3 0.6 reshape.84
  355.0 0.4 dynamic-update-slice
  355.3 22.7 %all-reduce = bf16[20800]{0:T(1024)(128)(2,1)} all-reduce(bf16[20800]{0:T(1024)(128)(2,1)S(1)} %dynamic-update-slice), channel_id=1, replica_groups=mesh['dp'=4,'tensor'=4,'section'=2] {'dp'}, use_global_device_ids=true, to_apply=%add | all-reduce | flops 20800 | bytes 83200
  378.1 101.9 %all-gather.2.cloned.1.call-done = bf16[800,4800]{1,0:T(8,128)(2,1)} async-done(((bf16[200,4800]{1,0:T(8,128)(2,1)}), bf16[800,4800]{1,0:T(8,128)(2,1)}) %all-gather.2.cloned.1.call-update) | async-done | bytes 7680016 | tf_op jit(solution)/shard_map/all_gather | solution.py:79
  480.0 6.9 %copy.23 = bf16[1,800,4800]{2,1,0:T(8,128)(2,1)} copy(bf16[1,800,4800]{2,1,0:T(8,128)(2,1)} %bitcast.39) | data formatting | bytes 15360000
  (29 shorter events, 0.3 us)
Async XLA Ops:
  7.2 273.1 %reduce-scatter.2.cloned.1.call-start = ((), (), s32[]{:S(2)}) async-start(), calls=%async_computation.1 | async-start | bytes 19456000 | tf_op jit(solution)/shard_map/reduce_scatter | solution.py:59
  17.0 0.9 copy-start
  17.1 324.0 %all-reduce.6.cloned.1.call-start = ((), (), s32[]{:S(2)}) async-start(), calls=%async_computation.3 | async-start | bytes 172032
  18.8 271.8 %copy-start.6 = (s32[4]{0:T(128)S(1)}, s32[4]{0:T(128)}, u32[]{:S(2)}) copy-start(s32[4]{0:T(128)} %constant.55.clone) | copy-start | bytes 52
  18.8 271.7 %copy-start.7 = (s32[4]{0:T(128)S(1)}, s32[4]{0:T(128)}, u32[]{:S(2)}) copy-start(s32[4]{0:T(128)} %constant.54.clone) | copy-start | bytes 52
  18.8 461.2 %all-gather.2.cloned.1.call-start = ((), (), s32[]{:S(2)}) async-start(), calls=%async_computation.2 | async-start | bytes 9728000 | tf_op jit(solution)/shard_map/all_gather | solution.py:79
  332.4 6.4 %copy-start.8 = (u32[32]{0:T(128)S(1)}, u32[32]{0:T(128)}, u32[]{:S(2)}) copy-start(u32[32]{0:T(128)} %constant.68) | copy-start | bytes 388
  332.4 8.3 %copy-start.1 = (f32[1,5200]{1,0:T(1,128)S(1)}, f32[1,5200]{1,0:T(1,128)}, u32[]{:S(2)}) copy-start(f32[1,5200]{1,0:T(1,128)} %param.17) | copy-start | bytes 62404
  332.4 8.4 %copy-start.2 = (f32[1,5200]{1,0:T(1,128)S(1)}, f32[1,5200]{1,0:T(1,128)}, u32[]{:S(2)}) copy-start(f32[1,5200]{1,0:T(1,128)} %param.19) | copy-start | bytes 62404
  332.4 8.4 %copy-start.3 = (f32[1,5200]{1,0:T(1,128)S(1)}, f32[1,5200]{1,0:T(1,128)}, u32[]{:S(2)}) copy-start(f32[1,5200]{1,0:T(1,128)} %param.18) | copy-start | bytes 62404
  332.4 9.5 %copy-start.4 = (s32[8]{0:T(128)S(1)}, s32[8]{0:T(128)}, u32[]{:S(2)}) copy-start(s32[8]{0:T(128)} %constant.57.clone) | copy-start | bytes 100
  332.5 9.5 %copy-start.5 = (s32[8]{0:T(128)S(1)}, s32[8]{0:T(128)}, u32[]{:S(2)}) copy-start(s32[8]{0:T(128)} %constant.56.clone) | copy-start | bytes 100
Sparse Core Ops, SparseCore 0:
  17.2 263.0 reduce-scatter.1
  282.7 34.9 all-reduce.5
  338.9 141.0 all-gather.1
where the time goes:
time: 494 us; the launch traced here: 493 us
  waiting for transfers between devices  363 us (73%)
  blocking collectives  74.8 us (15%)
  other arithmetic  29.3 us (6%)
  between operations  15.2 us (3%)
  local copies, waits for them, and re-layouts  10.6 us (2%)
    reduce_scatter x1, waiting for transfers between devices, local(): lax.psum_scatter(local_grad, 'dp', scatter_dimension=0, tiled=True)  261 us
    all_gather x1, waiting for transfers between devices, local(): lax.all_gather(master_new.astype(jnp.bfloat16), 'dp', axis=0, tiled=True)  102 us
    psum x1, blocking collectives, local(): lax.psum((weight_mat_sq, update_mat_sq), ('dp', 'tensor', 'section'))  41.4 us
    unnamed x1, blocking collectives  22.7 us
    psum x1, blocking collectives, local(): wsum_vec, usum_vec = lax.psum((weight_vec_sq, update_vec_sq), 'dp')  10.7 us
    reduce_sum x1, other arithmetic, local(): jnp.sum(direction * direction, axis=0)[None, :]  10.3 us
  transfers between devices with their start and end apart: 3, of which 2 were waited for; matrix products, arithmetic and copies ran while one was open for 5% of the time, Pallas kernels for 0%

commit v1 on v0

v1 whole, which is shorter than its diff:
```python
import functools

import jax
import jax.numpy as jnp
from jax import lax
from jax.experimental import pallas as pl
from jax.experimental.pallas import tpu as pltpu
from jax.sharding import PartitionSpec as P

D = 1600
FF = 6400
STEP = 10

BETA_ONE = 0.9
BETA_TWO = 0.999
EPSILON = 1e-06
LEARN_RATE = 0.25
DECAY_MAT = 0.01
LANES = 128
MESH = pl.DeviceIdType.MESH
GROUPS = ((3,), (2,), (0,), (1,))
AHEAD = 2


def adam_direction(gradient, master, first, second, decay):
    first_new = BETA_ONE * first + (1.0 - BETA_ONE) * gradient
    second_new = BETA_TWO * second + (1.0 - BETA_TWO) * gradient * gradient
    corr_one = 1.0 - BETA_ONE**STEP
    corr_two = 1.0 - BETA_TWO**STEP
    direction = first_new * (1.0 / corr_one) / (jnp.sqrt(second_new * (1.0 / corr_two)) + EPSILON)
    if decay:
        direction = direction + decay * master
    return (first_new, second_new, direction)


def plan(bounds, columns):
    tiles = -(-columns // LANES)

    def touched(group):
        found = set()
        for p in group:
            found |= set(range(bounds[p] // LANES, -(-bounds[p + 1] // LANES)))
        return found

    def ranges(found):
        out = []
        for t in sorted(found):
            if out and out[-1][1] == t:
                out[-1][1] = t + 1
            else:
                out.append([t, t + 1])
        return [(a * LANES, min(b * LANES, columns)) for a, b in out]

    reduced, seen = [], set()
    for group in GROUPS:
        reduced.append(ranges(touched(group) - seen))
        seen |= touched(group)
    assert len(seen) == tiles
    gathered, seen = [], set()
    for group in reversed(GROUPS):
        gathered.insert(0, ranges(touched(group) - seen))
        seen |= touched(group)
    return reduced, gathered


def over_tiles(lo, hi, body):
    full = (hi - lo) // LANES

    def step(j, carry):
        body(pl.ds(pl.multiple_of(lo + j * LANES, LANES), LANES), lo + j * LANES, LANES)
        return carry

    lax.fori_loop(0, full, step, 0)
    rest = hi - lo - full * LANES
    if rest:
        body(pl.ds(lo + full * LANES, rest), lo + full * LANES, rest)


def kernel(
    n, tensors, sections, bounds, bounds_vec, reduced, gathered,
    grad, gvec, mat_m, mat_f, mat_s, vec_m, vec_f, vec_s,
    out_w, out_m, out_f, out_s, out_gv, out_vm, out_vf, out_vs,
    got, own, master, first, second, direc, weights, csum_w, csum_u, vgot, vall, pmsg, pgot, dmsg, dgot,
    load_sem, rs_send, rs_recv, vs_send, vs_recv, vg_send, vg_recv, p_send, p_recv, d_send, d_recv,
    ag_send, ag_recv, out_sem, own_sem,
):
    me = lax.axis_index("dp")
    tensor, section = lax.axis_index("tensor"), lax.axis_index("section")
    groups = len(GROUPS)
    plane = tensors * sections
    spot = tensor * sections + section
    columns = own.shape[1]
    owned_vec = vec_m.shape[1]

    loads = [
        pltpu.make_async_copy(src, dst, load_sem.at[i])
        for i, (src, dst) in enumerate(((grad.at[me], own), (mat_m, master), (mat_f, first), (mat_s, second)))
    ]
    for load in loads:
        load.start()

    dp_peers = [{"dp": lax.rem(me + d, n)} for d in range(1, n)]
    plane_peers = []
    for d in range(1, plane):
        other = lax.rem(spot + d, plane)
        plane_peers.append({"tensor": other // sections, "section": lax.rem(other, sections)})
    barrier = pltpu.get_barrier_semaphore()
    for peer in dp_peers + plane_peers:
        pl.semaphore_signal(barrier, inc=1, device_id=peer, device_id_type=MESH)
    pl.semaphore_wait(barrier, len(dp_peers) + len(plane_peers))

    def remote(src, dst, send, recv, peer):
        return pltpu.make_async_remote_copy(
            src_ref=src, dst_ref=dst, send_sem=send, recv_sem=recv, device_id=peer, device_id_type=MESH
        )

    rs_index = []
    for g in range(groups):
        for k in range(len(reduced[g])):
            rs_index.append((g, k))
    ag_index = []
    for g in range(groups):
        for k in range(len(gathered[g])):
            ag_index.append((g, k))

    def rs_copies(g):
        copies = []
        for k, (lo, hi) in enumerate(reduced[g]):
            i = rs_index.index((g, k))
            for d in range(1, n):
                peer = dp_peers[d - 1]
                cols = pl.ds(lo, hi - lo)
                copies.append(remote(
                    grad.at[peer["dp"], :, cols], got.at[d - 1, :, cols],
                    rs_send.at[i, d - 1], rs_recv.at[i, d - 1], peer,
                ))
        return copies

    vec_copies = [
        remote(gvec.at[peer["dp"]], vgot.at[d], vs_send.at[d], vs_recv.at[d], peer) for d, peer in enumerate(dp_peers)
    ]
    for copy in vec_copies:
        copy.start()
    for g in range(min(AHEAD, groups)):
        for copy in rs_copies(g):
            copy.start()
    for load in loads:
        load.wait()

    vall_copies = [
        remote(vall.at[me], vall.at[me], vg_send.at[d], vg_recv.at[d], peer) for d, peer in enumerate(dp_peers)
    ]
    outs = []
    ratios = {}
    row = lax.broadcasted_iota(jnp.int32, (8, LANES), 0)
    lane = lax.broadcasted_iota(jnp.int32, (8, LANES), 1)

    def put(block, slot, weight_sq, update_sq):
        block = jnp.where((row == 0) & (lane == slot), weight_sq, block)
        return jnp.where((row == 1) & (lane == slot), update_sq, block)

    def pick(ratio, slot):
        return jnp.sum(jnp.where(lane[0:1] == slot, ratio, 0.0), axis=1, keepdims=True)

    def keep(src, dst):
        copy = pltpu.make_async_copy(src, dst, out_sem.at[len(outs)])
        copy.start()
        outs.append(copy)

    def hop(g, step, way, source, received):
        copies = []
        shard = source - step if way == 0 else source + step
        to = me + 1 if way == 0 else me - 1
        to = jnp.clip(to, 0, n - 1)
        shard = jnp.clip(shard, 0, n - 1)
        for k, (lo, hi) in enumerate(gathered[g]):
            i = ag_index.index((g, k))
            cols = pl.ds(lo, hi - lo)
            dst = out_w.at[shard, :, cols]
            src = weights.at[:, cols] if step == 0 and not received else dst
            copies.append(remote(src, dst, ag_send.at[i, way, step], ag_recv.at[i, way, step], {"dp": to}))
        return copies

    def leaving(step, way):
        if way == 0:
            return (me < n - 1) & (me >= step)
        return (me > 0) & (me + step <= n - 1)

    def reaching(step, way):
        if way == 0:
            return me - 1 - step >= 0
        return me + 1 + step <= n - 1

    def send_hop(g, step):
        for way in (0, 1):
            if step:
                @pl.when(reaching(step - 1, way))
                def _():
                    for copy in hop(g, step - 1, way, me - 1 if way == 0 else me + 1, True):
                        copy.wait_recv()
            if step < n - 1:
                @pl.when(leaving(step, way))
                def _():
                    for copy in hop(g, step, way, me, False):
                        copy.start()

    hops_done = [0] * groups

    def advance(g):
        if hops_done[g] <= n - 1:
            send_hop(g, hops_done[g])
            hops_done[g] += 1

    for g in range(groups):
        for copy in rs_copies(g):
            copy.wait()
        if g + AHEAD < groups:
            for copy in rs_copies(g + AHEAD):
                copy.start()
        for lo, hi in reduced[g]:
            def reduce_tile(cols, start, width):
                total = own[:, cols].astype(jnp.float32)
                for d in range(n - 1):
                    total = total + got[d, :, cols].astype(jnp.float32)
                old = master[:, cols]
                first_new, second_new, update = adam_direction(total, old, first[:, cols], second[:, cols], DECAY_MAT)
                first[:, cols] = first_new
                second[:, cols] = second_new
                direc[:, cols] = update
                csum_w[:, cols] = jnp.sum(old * old, axis=0, keepdims=True)
                csum_u[:, cols] = jnp.sum(update * update, axis=0, keepdims=True)

            over_tiles(lo, hi, reduce_tile)
        block = jnp.zeros((8, LANES), jnp.float32)
        column = lax.broadcasted_iota(jnp.int32, (1, columns), 1)
        for p in GROUPS[g]:
            inside = (column >= bounds[p]) & (column < bounds[p + 1])
            block = put(
                block, p,
                jnp.sum(jnp.where(inside, csum_w[...], 0.0), axis=1, keepdims=True),
                jnp.sum(jnp.where(inside, csum_u[...], 0.0), axis=1, keepdims=True),
            )
        pmsg[g] = block
        plane_copies = [
            remote(pmsg.at[g], pgot.at[g, d], p_send.at[g, d], p_recv.at[g, d], peer)
            for d, peer in enumerate(plane_peers)
        ]
        for copy in plane_copies:
            copy.start()
        for lo, hi in reduced[g]:
            cols = pl.ds(lo, hi - lo)
            keep(first.at[:, cols], out_f.at[:, cols])
            keep(second.at[:, cols], out_s.at[:, cols])
        if g == 0:
            for copy in vec_copies:
                copy.wait()
            total_v = gvec[me]
            for d in range(n - 1):
                total_v = total_v + vgot[d]
            old_v = vec_m[...]
            first_v, second_v, update_v = adam_direction(total_v, old_v, vec_f[...], vec_s[...], 0.0)
            out_vf[...] = first_v
            out_vs[...] = second_v
            index = me * owned_vec + lax.broadcasted_iota(jnp.int32, (1, owned_vec), 1)
            extra = jnp.zeros((8, LANES), jnp.float32)
            for p in range(len(bounds_vec) - 1):
                inside = (index >= bounds_vec[p]) & (index < bounds_vec[p + 1])
                extra = put(
                    extra, 4 + p,
                    jnp.sum(jnp.where(inside, old_v * old_v, 0.0), axis=1, keepdims=True),
                    jnp.sum(jnp.where(inside, update_v * update_v, 0.0), axis=1, keepdims=True),
                )
        for d, copy in enumerate(plane_copies):
            copy.wait()
            block = block + pgot[g, d]
        if g == 0:
            block = block + extra
        dmsg[g] = block
        dp_copies = [
            remote(dmsg.at[g], dgot.at[g, d], d_send.at[g, d], d_recv.at[g, d], peer) for d, peer in enumerate(dp_peers)
        ]
        for copy in dp_copies:
            copy.start()
        for earlier in range(g):
            advance(earlier)
        for d, copy in enumerate(dp_copies):
            copy.wait()
            block = block + dgot[g, d]
        ratio = jnp.sqrt(block[0:1]) / jnp.sqrt(block[1:2])
        for p in GROUPS[g]:
            ratios[p] = LEARN_RATE * pick(ratio, p)
        for lo, hi in gathered[g]:
            def apply_tile(cols, start, width):
                position = start + lax.broadcasted_iota(jnp.int32, (1, width), 1)
                scale = jnp.zeros((1, width), jnp.float32)
                for p, value in ratios.items():
                    scale = jnp.where((position >= bounds[p]) & (position < bounds[p + 1]), value, scale)
                new = master[:, cols] - scale * direc[:, cols]
                master[:, cols] = new
                weights[:, cols] = new.astype(jnp.bfloat16)

            over_tiles(lo, hi, apply_tile)
        advance(g)
        for k, (lo, hi) in enumerate(gathered[g]):
            cols = pl.ds(lo, hi - lo)
            keep(weights.at[:, cols], out_w.at[me, :, cols])
            keep(master.at[:, cols], out_m.at[:, cols])
        if g == 0:
            scale_v = jnp.zeros((1, owned_vec), jnp.float32)
            for p in range(len(bounds_vec) - 1):
                inside = (index >= bounds_vec[p]) & (index < bounds_vec[p + 1])
                scale_v = jnp.where(inside, LEARN_RATE * pick(ratio, 4 + p), scale_v)
            new_v = old_v - scale_v * update_v
            out_vm[...] = new_v
            vall[me] = new_v
            for copy in vall_copies:
                copy.start()
    for _ in range(n):
        for g in range(groups):
            advance(g)
    for d, copy in enumerate(vall_copies):
        copy.wait_send()
        origin = lax.rem(me + n - 1 - d, n)
        remote(vall.at[origin], vall.at[origin], vg_send.at[d], vg_recv.at[d], dp_peers[d]).wait_recv()
    out_gv[...] = vall[...]
    for g in range(groups):
        for step in range(n - 1):
            for way in (0, 1):
                @pl.when(leaving(step, way))
                def _():
                    for copy in hop(g, step, way, me, False):
                        copy.wait_send()
    for copy in outs:
        copy.wait()


def local(grad_mat, grad_vec, master_mat, first_mat, second_mat, master_vec, first_vec, second_vec):
    n, tensors, sections = (lax.axis_size(name) for name in ("dp", "tensor", "section"))
    section_rows, columns = grad_mat.shape[2:]
    rows = section_rows // n
    state_shape = master_mat.shape
    owned_vec = master_vec.shape[1]
    bounds = (0, 3 * D // tensors, 4 * D // tensors, (4 * D + FF) // tensors, columns)
    bounds_vec = (0, D, 2 * D, 5 * D, 6 * D, 7 * D, 8 * D, 8 * D + FF, 9 * D + FF)
    reduced, gathered = plan(bounds, columns)
    groups = len(GROUPS)
    n_rs, n_ag = sum(map(len, reduced)), sum(map(len, gathered))
    plane = tensors * sections
    f32, bf16 = jnp.float32, jnp.bfloat16
    any_space, vmem = pl.BlockSpec(memory_space=pl.ANY), pl.BlockSpec(memory_space=pltpu.VMEM)
    dma = pltpu.SemaphoreType.DMA
    mat = jax.ShapeDtypeStruct((rows, columns), f32)
    vec = jax.ShapeDtypeStruct((1, owned_vec), f32)
    weights, new_m, new_f, new_s, gathered_v, new_vm, new_vf, new_vs = pl.pallas_call(
        functools.partial(kernel, n, tensors, sections, bounds, bounds_vec, reduced, gathered),
        out_shape=[
            jax.ShapeDtypeStruct((n, rows, columns), bf16), mat, mat, mat,
            jax.ShapeDtypeStruct((n, 1, owned_vec), f32), vec, vec, vec,
        ],
        in_specs=[any_space, vmem, any_space, any_space, any_space, vmem, vmem, vmem],
        out_specs=[any_space, any_space, any_space, any_space, vmem, vmem, vmem, vmem],
        scratch_shapes=[
            pltpu.VMEM((n - 1, rows, columns), bf16),
            pltpu.VMEM((rows, columns), bf16),
            pltpu.VMEM((rows, columns), f32),
            pltpu.VMEM((rows, columns), f32),
            pltpu.VMEM((rows, columns), f32),
            pltpu.VMEM((rows, columns), f32),
            pltpu.VMEM((rows, columns), bf16),
            pltpu.VMEM((1, columns), f32),
            pltpu.VMEM((1, columns), f32),
            pltpu.VMEM((n - 1, 1, owned_vec), f32),
            pltpu.VMEM((n, 1, owned_vec), f32),
            pltpu.VMEM((groups, 8, LANES), f32),
            pltpu.VMEM((groups, plane - 1, 8, LANES), f32),
            pltpu.VMEM((groups, 8, LANES), f32),
            pltpu.VMEM((groups, n - 1, 8, LANES), f32),
            dma((4,)), dma((n_rs, n - 1)), dma((n_rs, n - 1)), dma((n - 1,)), dma((n - 1,)), dma((n - 1,)),
            dma((n - 1,)), dma((groups, plane - 1)), dma((groups, plane - 1)), dma((groups, n - 1)),
            dma((groups, n - 1)), dma((n_ag, 2, n - 1)), dma((n_ag, 2, n - 1)), dma((2 * n_rs + 2 * n_ag,)), dma((1,)),
        ],
        compiler_params=pltpu.CompilerParams(collective_id=0, has_side_effects=True, vmem_limit_bytes=56 << 20),
        cost_estimate=pl.CostEstimate(flops=40 * rows * columns, bytes_accessed=36 * rows * columns, transcendentals=0),
    )(
        grad_mat.reshape(n, rows, columns),
        grad_vec.astype(f32).reshape(n, 1, owned_vec),
        master_mat.reshape(rows, columns),
        first_mat.reshape(rows, columns),
        second_mat.reshape(rows, columns),
        master_vec, first_vec, second_vec,
    )
    return (
        weights.reshape(1, section_rows, columns),
        gathered_v.reshape(n * owned_vec).astype(bf16),
        new_m.reshape(state_shape),
        new_f.reshape(state_shape),
        new_s.reshape(state_shape),
        new_vm, new_vf, new_vs,
    )


def solution(mesh):
    state = P("tensor", "section", "dp", None, None)
    in_specs = (
        P("dp", "tensor", "section", None), P("dp", None), state, state, state, P("dp", None), P("dp", None), P("dp", None),
    )
    out_specs = (
        P("tensor", "section", None), P(), state, state, state, P("dp", None), P("dp", None), P("dp", None),
    )
    return jax.shard_map(local, mesh=mesh, in_specs=in_specs, out_specs=out_specs, check_vma=False)
```

time: 494 us -> 329 us (0.67)
  waiting for transfers between devices: 363 us -> 0 us
  Pallas kernels: 0 us -> 306 us
  blocking collectives: 74.8 us -> 0 us
  other arithmetic: 29.3 us -> 2.24 us
  between operations: 15.2 us -> 0.66 us
  local copies, waits for them, and re-layouts: 10.6 us -> 19.3 us
    pallas_call x0 -> x1, Pallas kernels: none -> 306 us  [local(): pl.pallas_call(functools.partial(kernel, n, tensors, sections, bounds, bo...]
    reduce_scatter x1 -> x0, waiting for transfers between devices: 261 us -> none  [local(): lax.psum_scatter(local_grad, 'dp', scatter_dimension=0, tiled=True)]
    all_gather x1 -> x0, waiting for transfers between devices: 102 us -> none  [local(): lax.all_gather(master_new.astype(jnp.bfloat16), 'dp', axis=0, tiled=True)]
    psum x2 -> x0, blocking collectives: 52.1 us -> none  [the longest x1 41.4 us: local(): lax.psum((weight_mat_sq, update_mat_sq), ('dp', 'tensor', 'section'))]
    unnamed x1 -> x0, blocking collectives: 22.7 us -> none
    reduce_sum x5 -> x0, other arithmetic: 11.2 us -> none  [the longest x1 10.3 us: local(): jnp.sum(direction * direction, axis=0)[None, :]]
    convert_element_type x3 -> x1, other arithmetic: 10.7 us -> 1.13 us  [local(): gathered_v.reshape(n * owned_vec).astype(bf16)]
    unnamed x22 -> x19, local copies, waits for them, and re-layouts: 8.72 us -> 17.8 us
  transfers between devices with their start and end apart: 3 -> 0, of which waited for: 2 -> 0; matrix products, arithmetic and copies ran while one was open for 5% -> 0% of each run, Pallas kernels for 0% -> 0%
where the time goes in v1:
time: 329 us
  Pallas kernels  306 us (93%)
  local copies, waits for them, and re-layouts  19.3 us (6%)
    pallas_call x1, Pallas kernels, local(): pl.pallas_call(functools.partial(kernel, n, tensors, sections, bounds, bo...  306 us
    unnamed x19, local copies, waits for them, and re-layouts  17.8 us

profile of v1, /device:TPU:0, one launch (start us, length us, event | category | flops | bytes accessed | tf_op | source)
XLA Modules:
  0.0 328.6 jit_solution(3745041103882699193)
XLA Ops:
  0.6 1.1 convert_reduce_fusion.1
  1.8 0.8 reshape.58.gvec
  2.5 306.4 %shard_map.143 = (bf16[4,200,4800]{2,1,0:T(8,128)(2,1)}, f32[200,4800]{1,0:T(8,128)}, f32[200,4800]{1,0:T(8,128)}, f32[200,4800]{1,0:T(8,128)}, f32[4,1,5200]{2,...) custom-call(bf16[4,200,4800]{2,1,0:T(8,128)(2,1)} %bitcast.8, f32[4,1,5200]{2,1,0:T(1,128)} %reshape.58.gvec, ...), custom_call_target="tpu_custom_call" | custom-call | flops 38400000 | bytes 34560000 | tf_op jit(solution)/shard_map/pallas_call | solution.py:354
  309.0 1.1 convert_reduce_fusion
  310.1 0.7 convert_element_type.8
  310.8 0.0 copy-start.2
  310.8 7.1 %copy.23 = bf16[1,800,4800]{2,1,0:T(8,128)(2,1)} copy(bf16[1,800,4800]{2,1,0:T(8,128)(2,1)} %bitcast.9) | data formatting | bytes 15360000
  317.9 0.0 copy-done.2
  317.9 0.0 copy-start.1
  317.9 2.0 copy.24
  319.9 1.5 copy-done.1
  321.4 0.0 copy-start
  321.4 2.0 copy.25
  323.4 1.5 copy-done
  324.9 0.0 copy-start.5
  324.9 0.0 copy-start.4
  324.9 0.0 copy-start.3
  324.9 1.9 copy.26
  326.8 0.0 copy-done.5
  326.8 0.6 copy.27
  327.4 0.0 copy-done.4
  327.4 0.6 copy.28
  328.0 0.0 copy-done.3
  328.0 0.6 copy.29
Async XLA Ops:
  310.8 7.1 %copy-start.2 = (f32[200,4800]{1,0:T(8,128)S(1)}, f32[200,4800]{1,0:T(8,128)}, u32[]{:S(2)}) copy-start(f32[200,4800]{1,0:T(8,128)} %get-tuple-element.18) | copy-start | bytes 11520004
  317.9 3.5 %copy-start.1 = (f32[200,4800]{1,0:T(8,128)S(1)}, f32[200,4800]{1,0:T(8,128)}, u32[]{:S(2)}) copy-start(f32[200,4800]{1,0:T(8,128)} %get-tuple-element.19) | copy-start | bytes 11520004
  321.4 3.5 %copy-start = (f32[200,4800]{1,0:T(8,128)S(1)}, f32[200,4800]{1,0:T(8,128)}, u32[]{:S(2)}) copy-start(f32[200,4800]{1,0:T(8,128)} %get-tuple-element.20) | copy-start | bytes 11520004
  324.9 1.9 copy-start.5
  324.9 2.5 copy-start.4
  324.9 3.1 copy-start.3

commit v2 on v1

--- a/solution.py
+++ b/solution.py
@@ -18,8 +18,10 @@
 DECAY_MAT = 0.01
 LANES = 128
 MESH = pl.DeviceIdType.MESH
-GROUPS = ((3,), (2,), (0,), (1,))
+GROUPS = ((0,), (3,), (2,), (1,))
+PIECE = 3
 AHEAD = 2
+PART = 4
 
 
 def adam_direction(gradient, master, first, second, decay):
@@ -51,14 +53,22 @@
                 out.append([t, t + 1])
         return [(a * LANES, min(b * LANES, columns)) for a, b in out]
 
+    def cut(found, size):
+        out = []
+        for lo, hi in ranges(found):
+            count = -(-(hi - lo) // (size * LANES))
+            step = -(-(hi - lo) // (count * LANES)) * LANES
+            out += [(a, min(a + step, hi)) for a in range(lo, hi, step)]
+        return out
+
     reduced, seen = [], set()
     for group in GROUPS:
-        reduced.append(ranges(touched(group) - seen))
+        reduced.append(cut(touched(group) - seen, PIECE))
         seen |= touched(group)
     assert len(seen) == tiles
     gathered, seen = [], set()
     for group in reversed(GROUPS):
-        gathered.insert(0, ranges(touched(group) - seen))
+        gathered.insert(0, cut(touched(group) - seen, PART))
         seen |= touched(group)
     return reduced, gathered
 
@@ -114,35 +124,26 @@
             src_ref=src, dst_ref=dst, send_sem=send, recv_sem=recv, device_id=peer, device_id_type=MESH
         )
 
-    rs_index = []
-    for g in range(groups):
-        for k in range(len(reduced[g])):
-            rs_index.append((g, k))
-    ag_index = []
-    for g in range(groups):
-        for k in range(len(gathered[g])):
-            ag_index.append((g, k))
-
-    def rs_copies(g):
-        copies = []
-        for k, (lo, hi) in enumerate(reduced[g]):
-            i = rs_index.index((g, k))
-            for d in range(1, n):
-                peer = dp_peers[d - 1]
-                cols = pl.ds(lo, hi - lo)
-                copies.append(remote(
-                    grad.at[peer["dp"], :, cols], got.at[d - 1, :, cols],
-                    rs_send.at[i, d - 1], rs_recv.at[i, d - 1], peer,
-                ))
-        return copies
+    pieces = [(g, lo, hi) for g in range(groups) for lo, hi in reduced[g]]
+    parts = [(g, lo, hi) for g in range(groups) for lo, hi in gathered[g]]
+
+    def rs_copies(i):
+        _, lo, hi = pieces[i]
+        cols = pl.ds(lo, hi - lo)
+        return [
+            remote(
+                grad.at[peer["dp"], :, cols], got.at[d, :, cols], rs_send.at[i, d], rs_recv.at[i, d], peer
+            )
+            for d, peer in enumerate(dp_peers)
+        ]
 
     vec_copies = [
         remote(gvec.at[peer["dp"]], vgot.at[d], vs_send.at[d], vs_recv.at[d], peer) for d, peer in enumerate(dp_peers)
     ]
     for copy in vec_copies:
         copy.start()
-    for g in range(min(AHEAD, groups)):
-        for copy in rs_copies(g):
+    for i in range(min(AHEAD, len(pieces))):
+        for copy in rs_copies(i):
             copy.start()
     for load in loads:
         load.wait()
@@ -167,19 +168,16 @@
         copy.start()
         outs.append(copy)
 
-    def hop(g, step, way, source, received):
-        copies = []
+    def hop(i, step, way, source, received):
         shard = source - step if way == 0 else source + step
         to = me + 1 if way == 0 else me - 1
         to = jnp.clip(to, 0, n - 1)
         shard = jnp.clip(shard, 0, n - 1)
-        for k, (lo, hi) in enumerate(gathered[g]):
-            i = ag_index.index((g, k))
-            cols = pl.ds(lo, hi - lo)
-            dst = out_w.at[shard, :, cols]
-            src = weights.at[:, cols] if step == 0 and not received else dst
-            copies.append(remote(src, dst, ag_send.at[i, way, step], ag_recv.at[i, way, step], {"dp": to}))
-        return copies
+        _, lo, hi = parts[i]
+        cols = pl.ds(lo, hi - lo)
+        dst = out_w.at[shard, :, cols]
+        src = weights.at[:, cols] if step == 0 and not received else dst
+        return remote(src, dst, ag_send.at[i, way, step], ag_recv.at[i, way, step], {"dp": to})
 
     def leaving(step, way):
         if way == 0:
@@ -191,33 +189,32 @@
             return me - 1 - step >= 0
         return me + 1 + step <= n - 1
 
-    def send_hop(g, step):
+    def send_hop(i, step):
         for way in (0, 1):
             if step:
                 @pl.when(reaching(step - 1, way))
                 def _():
-                    for copy in hop(g, step - 1, way, me - 1 if way == 0 else me + 1, True):
-                        copy.wait_recv()
+                    hop(i, step - 1, way, me - 1 if way == 0 else me + 1, True).wait_recv()
             if step < n - 1:
                 @pl.when(leaving(step, way))
                 def _():
-                    for copy in hop(g, step, way, me, False):
-                        copy.start()
-
-    hops_done = [0] * groups
-
-    def advance(g):
-        if hops_done[g] <= n - 1:
-            send_hop(g, hops_done[g])
-            hops_done[g] += 1
-
-    for g in range(groups):
-        for copy in rs_copies(g):
+                    hop(i, step, way, me, False).start()
+
+    hops_done = {}
+
+    def advance_all():
+        for i in hops_done:
+            if hops_done[i] < n:
+                send_hop(i, hops_done[i])
+                hops_done[i] += 1
+
+    for number, (g, piece_lo, piece_hi) in enumerate(pieces):
+        for copy in rs_copies(number):
             copy.wait()
-        if g + AHEAD < groups:
-            for copy in rs_copies(g + AHEAD):
+        if number + AHEAD < len(pieces):
+            for copy in rs_copies(number + AHEAD):
                 copy.start()
-        for lo, hi in reduced[g]:
+        for lo, hi in ((piece_lo, piece_hi),):
             def reduce_tile(cols, start, width):
                 total = own[:, cols].astype(jnp.float32)
                 for d in range(n - 1):
@@ -231,6 +228,12 @@
                 csum_u[:, cols] = jnp.sum(update * update, axis=0, keepdims=True)
 
             over_tiles(lo, hi, reduce_tile)
+            cols = pl.ds(lo, hi - lo)
+            keep(first.at[:, cols], out_f.at[:, cols])
+            keep(second.at[:, cols], out_s.at[:, cols])
+        if number + 1 < len(pieces) and pieces[number + 1][0] == g:
+            advance_all()
+            continue
         block = jnp.zeros((8, LANES), jnp.float32)
         column = lax.broadcasted_iota(jnp.int32, (1, columns), 1)
         for p in GROUPS[g]:
@@ -247,10 +250,6 @@
         ]
         for copy in plane_copies:
             copy.start()
-        for lo, hi in reduced[g]:
-            cols = pl.ds(lo, hi - lo)
-            keep(first.at[:, cols], out_f.at[:, cols])
-            keep(second.at[:, cols], out_s.at[:, cols])
         if g == 0:
             for copy in vec_copies:
                 copy.wait()
@@ -281,8 +280,7 @@
         ]
         for copy in dp_copies:
             copy.start()
-        for earlier in range(g):
-            advance(earlier)
+        advance_all()
         for d, copy in enumerate(dp_copies):
             copy.wait()
             block = block + dgot[g, d]
@@ -300,8 +298,10 @@
                 weights[:, cols] = new.astype(jnp.bfloat16)
 
             over_tiles(lo, hi, apply_tile)
-        advance(g)
-        for k, (lo, hi) in enumerate(gathered[g]):
+            i = parts.index((g, lo, hi))
+            send_hop(i, 0)
+            hops_done[i] = 1
+        for lo, hi in gathered[g]:
             cols = pl.ds(lo, hi - lo)
             keep(weights.at[:, cols], out_w.at[me, :, cols])
             keep(master.at[:, cols], out_m.at[:, cols])
@@ -316,22 +316,44 @@
             for copy in vall_copies:
                 copy.start()
     for _ in range(n):
-        for g in range(groups):
-            advance(g)
+        advance_all()
     for d, copy in enumerate(vall_copies):
         copy.wait_send()
         origin = lax.rem(me + n - 1 - d, n)
         remote(vall.at[origin], vall.at[origin], vg_send.at[d], vg_recv.at[d], dp_peers[d]).wait_recv()
     out_gv[...] = vall[...]
-    for g in range(groups):
+    for i in range(len(parts)):
         for step in range(n - 1):
             for way in (0, 1):
                 @pl.when(leaving(step, way))
                 def _():
-                    for copy in hop(g, step, way, me, False):
-                        copy.wait_send()
+                    hop(i, step, way, me, False).wait_send()
     for copy in outs:
         copy.wait()
+
+
+def hand_over(*refs):
+    count = (len(refs) - 2) // 3
+    load_sem, store_sem = refs[-2:]
+    loads, stores = [], []
+    for i in range(count):
+        src, dst, buf = refs[i], refs[count + i], refs[2 * count + i]
+        total = src.shape[0]
+        size = total if total < 16 else -(-total // (4 * 16)) * 16
+        if src.dtype == jnp.bfloat16:
+            size = 1
+        for lo in range(0, total, size):
+            part = pl.ds(lo, min(size, total - lo))
+            k = len(loads)
+            loads.append(pltpu.make_async_copy(src.at[part], buf.at[part], load_sem.at[k]))
+            stores.append(pltpu.make_async_copy(buf.at[part], dst.at[part], store_sem.at[k]))
+    for load in loads:
+        load.start()
+    for load, store in zip(loads, stores):
+        load.wait()
+        store.start()
+    for store in stores:
+        store.wait()
 
 
 def local(grad_mat, grad_vec, master_mat, first_mat, second_mat, master_vec, first_vec, second_vec):
@@ -389,6 +411,16 @@
         second_mat.reshape(rows, columns),
         master_vec, first_vec, second_vec,
     )
+    handed = (weights, new_m, new_f, new_s, new_vm, new_vf, new_vs)
+    weights, new_m, new_f, new_s, new_vm, new_vf, new_vs = pl.pallas_call(
+        hand_over,
+        out_shape=[jax.ShapeDtypeStruct(a.shape, a.dtype) for a in handed],
+        in_specs=[any_space] * len(handed),
+        out_specs=[any_space] * len(handed),
+        scratch_shapes=[pltpu.VMEM(a.shape, a.dtype) for a in handed] + [dma((n + 16,)), dma((n + 16,))],
+        compiler_params=pltpu.CompilerParams(vmem_limit_bytes=60 << 20),
+        cost_estimate=pl.CostEstimate(flops=0, bytes_accessed=40 * rows * columns, transcendentals=0),
+    )(*handed)
     return (
         weights.reshape(1, section_rows, columns),
         gathered_v.reshape(n * owned_vec).astype(bf16),

time: 329 us -> 314 us (0.954)
  local copies, waits for them, and re-layouts: 19.3 us -> 1.53 us
  Pallas kernels: 306 us -> 310 us
    unnamed x19 -> x2, local copies, waits for them, and re-layouts: 17.8 us -> 0.01 us
    pallas_call x0 -> x1, Pallas kernels: none -> 13.8 us  [local(): pl.pallas_call(hand_over, out_shape=[jax.ShapeDtypeStruct(a.shape, a.dtyp...]
    pallas_call x1, Pallas kernels: 306 us -> 296 us  [local(): pl.pallas_call(functools.partial(kernel, n, tensors, sections, bounds, bo...]
where the time goes in v2:
time: 314 us
  Pallas kernels  310 us (99%)
    pallas_call x1, Pallas kernels, local(): pl.pallas_call(functools.partial(kernel, n, tensors, sections, bounds, bo...  296 us
    pallas_call x1, Pallas kernels, local(): pl.pallas_call(hand_over, out_shape=[jax.ShapeDtypeStruct(a.shape, a.dtyp...  13.8 us

profile of v2, /device:TPU:0, one launch (start us, length us, event | category | flops | bytes accessed | tf_op | source)
XLA Modules:
  0.0 313.6 jit_solution(4529595918929205685)
XLA Ops:
  0.6 1.1 convert_reduce_fusion.1
  1.8 0.8 reshape.58.gvec
  2.5 296.3 %shard_map.143 = (bf16[4,200,4800]{2,1,0:T(8,128)(2,1)}, f32[200,4800]{1,0:T(8,128)}, f32[200,4800]{1,0:T(8,128)}, f32[200,4800]{1,0:T(8,128)}, f32[4,1,5200]{2,...) custom-call(bf16[4,200,4800]{2,1,0:T(8,128)(2,1)} %bitcast.8, f32[4,1,5200]{2,1,0:T(1,128)} %reshape.58.gvec, ...), custom_call_target="tpu_custom_call" | custom-call | flops 38400000 | bytes 34560000 | tf_op jit(solution)/shard_map/pallas_call | solution.py:376
  298.8 0.0 copy-start
  298.8 13.8 %shard_map.144 = (bf16[4,200,4800]{2,1,0:T(8,128)(2,1)}, f32[200,4800]{1,0:T(8,128)}, f32[200,4800]{1,0:T(8,128)}, f32[200,4800]{1,0:T(8,128)}, f32[1,5200]{1,0:...) custom-call(bf16[4,200,4800]{2,1,0:T(8,128)(2,1)} %get-tuple-element.23.refs_0_, f32[200,4800]{1,0:T(8,128)} %get-tuple-element.24.refs_1_, ...), custom_call_target="tpu_custom_call" | custom-call | bytes 38400000 | tf_op jit(solution)/shard_map/pallas_call | solution.py:415
  312.6 0.0 copy-done
  312.6 0.2 convert_reduce_fusion
  312.9 0.7 convert_element_type.8
Async XLA Ops:
  298.8 13.8 %copy-start = (f32[4,1,5200]{2,1,0:T(1,128)S(1)}, f32[4,1,5200]{2,1,0:T(1,128)}, u32[]{:S(2)}) copy-start(f32[4,1,5200]{2,1,0:T(1,128)} %get-tuple-element.31) | copy-start | bytes 249604
